TPU v7x, 32 devices: a whole 2x2x4 slice. The times are simulated.
32 devices in a mesh: group: 4 (over y, x), cluster: 8 (over z, core).
Axes of the slice: x: 2, y: 2, z: 4, core: 2. Of those that a mesh axis runs over, the one named last changes fastest.
Arguments:
- charges: float32 [262144, 128], P(('group', 'cluster')), may hold values from -6 to 6
- leaf_size: int32 [1024], P(('group', 'cluster')), may hold values from 1 to 256, 196608 in all
- leaf_basis: float32 [1024, 64, 256], P(('group', 'cluster')), may hold values from -0.375 to 0.375
- leaf_transfer: float32 [1024, 64, 64], P(('group', 'cluster')), may hold values from -0.375 to 0.375
- mid_transfer: float32 [256, 64, 64], P(('group', 'cluster')), may hold values from -0.25 to 0.25
- leaf_parent: int32 [1024], P(('group', 'cluster')), may hold values from 0 to 7, as said below
- send_leaf: int32 [2048], P(('group', 'cluster')), may hold values from 0 to 32, as said below
- pair_leaf: int32 [1024, 12], P(('group', 'cluster')), may hold values from 0 to 64, as said below
- leaf_coupling: float32 [1024, 64, 768], P(('group', 'cluster')), may hold values from -0.21875 to 0.21875
- send_mid: int32 [2048], P(('group', 'cluster')), may hold values from 0 to 8, as said below
- pair_mid: int32 [256, 32], P(('group', 'cluster')), may hold values from 0 to 64, as said below
- mid_coupling: float32 [256, 64, 2048], P(('group', 'cluster')), may hold values from -0.125 to 0.125
- top_pairs: int32 [32, 4], P('group'), may hold values from 0 to 32, as said below
- top_coupling: float32 [32, 64, 256], P('group'), may hold values from -0.375 to 0.375
Outputs:
- far_field: float32 [262144, 128], P(('group', 'cluster'))
Inputs may be any that keep to these rules, and one draw needn't show every extreme that they name: `send_leaf`: entry (d * 32 + r) * 2 + j is the leaf, local to device d, whose block d puts in slot j for device r, or 32 for an empty slot; the leaves in one sender's slots to one receiver are distinct; some receiver has every slot from every sender filled. `pair_leaf`: row t names leaf t's admissible partners as positions 2 * d + j among the slots its owner receives, filled slots only and distinct within a row, or 64 for no partner; every filled slot is named by some row of its receiver. `send_mid`: as send_leaf, for level-one clusters: local indices below 8, 8 for an empty slot; some receiver has every slot from every sender filled. `pair_mid`: as pair_leaf, for level-one clusters; every filled slot is named by some row of its receiver. `leaf_parent`: every level-one cluster of a device is the parent of at least one of its leaves. `top_pairs`: row o names coarse clusters other than o, distinct within a row, at least one a row, or 32 for no partner.
All inputs are finite; a program needn't handle non-finite values. No bound on the sum of `leaf_size` on one device may be relied on, other than what follows from the above.
Results may differ from a plain program's by a relative error of at most 0.000062.
Values sent between devices are 32-bit elements; how exact they have to be, the bound alone decides.
No kernel may reach another device: no remote copies, remote signals or barrier semaphores. Data moves between devices by JAX's collectives and lax.ppermute only.
A program may use at most 128 MiB of HBM per device.

v0:
```python
import functools

import jax
import jax.numpy as jnp
from jax import lax
from jax.experimental import pallas as pl
from jax.experimental.pallas import tpu as pltpu
from jax.sharding import PartitionSpec as P

AXES = ("group", "cluster")
MIB = 1024 * 1024


def params(size):
    return pltpu.CompilerParams(vmem_limit_bytes=size)


def cost(flops, size):
    return pl.CostEstimate(flops=flops, bytes_accessed=size, transcendentals=0)


def whole(shape):
    return pl.BlockSpec(shape, lambda i, *_: (0,) * len(shape), pipeline_mode=pl.Buffered(1))


def first(group, *rest):
    return pl.BlockSpec((group,) + rest, lambda i, *_: (i,) + (0,) * len(rest))


def split(x):
    high = x.astype(jnp.bfloat16)
    low = (x - high.astype(jnp.float32)).astype(jnp.bfloat16)
    return high, low


def rows_of(x):
    return jnp.concatenate(split(x), axis=0)


def lanes_of(x):
    return jnp.concatenate(split(x), axis=1)


def dot(a, b):
    return lax.dot_general(a, b, (((1,), (0,)), ((), ())), preferred_element_type=jnp.float32)


def fold(product):
    m, n = product.shape[0] // 2, product.shape[1] // 2
    return product[:m, :n] + (product[:m, n:] + product[m:, :n] + product[m:, n:])


def deep_dot(a, b):
    high, low = split(b)
    return dot(jnp.concatenate([a, a], axis=1), jnp.concatenate([high, high, low, low], axis=0))


def up_kernel(
    sizes, size, parent, slots, group_at, lane_at, charges, basis, transfer, mid_transfer, send, coef, up,
    *messages
):
    step = pl.program_id(0)
    group, rank, points = basis.shape
    mids = mid_transfer.shape[0]
    ports = up.shape[1]

    @pl.when(step == 0)
    def _():
        up[: mids * rank, :] = jnp.zeros((mids * rank, ports), jnp.float32)
        up[(mids + 1) * rank :, :] = jnp.zeros((up.shape[0] - (mids + 1) * rank, ports), jnp.float32)
        for row in range(send.shape[0]):
            spot = (mids + 1) * rank + row
            up[spot : spot + 1, : send.shape[1]] = send[row : row + 1, :].astype(jnp.float32)

    point = lax.broadcasted_iota(jnp.int32, (points, ports), 0)
    values = []
    for g in range(group):
        block = jnp.where(
            point < size[step * group + g], charges[g * points : (g + 1) * points, :], 0.0
        )
        values.append(fold(dot(rows_of(basis[g]), lanes_of(block))))
    for g in range(group):
        coef[g] = values[g]
    moved = [fold(dot(rows_of(transfer[g]), lanes_of(values[g]))) for g in range(group)]
    for g in range(group):
        where = pl.ds(pl.multiple_of(parent[step * group + g] * rank, rank), rank)
        up[where, :] += moved[g]

    @pl.when(step == pl.num_programs(0) - 1)
    def _():
        terms = [
            fold(dot(rows_of(mid_transfer[c]), lanes_of(up[c * rank : (c + 1) * rank, :])))
            for c in range(mids)
        ]
        while len(terms) > 1:
            terms = [sum(terms[i : i + 2]) for i in range(0, len(terms), 2)]
        up[mids * rank : (mids + 1) * rank, :] = terms[0]
        per_cluster, per_pair = sizes
        for d, message in enumerate(messages):
            for side in range(2):
                receiver = (group_at[0] ^ d) * per_cluster + (lane_at[0] ^ side)
                for j in range(per_pair):
                    block = jnp.clip(slots[receiver * per_pair + j], 0, mids - 1)
                    source = pl.ds(pl.multiple_of(block * rank, rank), rank)
                    message[(1 - side) * (per_pair + 1) + j] = up[source, :]
            message[per_pair] = terms[0]


def up_sweep(
    sizes, groups, group_at, lane_at, charges, leaf_size, basis, transfer, mid_transfer, leaf_parent, slots
):
    leaves, rank, points = basis.shape
    ports = charges.shape[1]
    mids = mid_transfer.shape[0]
    group = 8
    send_mid = slots.reshape(-1, min(slots.shape[0], ports))
    up_rows = (mids + 1) * rank + -(-send_mid.shape[0] // 8) * 8
    message = (2 * sizes[1] + 1, rank, ports)
    return pl.pallas_call(
        functools.partial(up_kernel, sizes),
        grid_spec=pltpu.PrefetchScalarGridSpec(
            num_scalar_prefetch=5,
            grid=(leaves // group,),
            in_specs=[
                first(group * points, ports),
                first(group, rank, points),
                first(group, rank, rank),
                whole(mid_transfer.shape),
                whole(send_mid.shape),
            ],
            out_specs=[first(group, rank, ports), whole((up_rows, ports))] + [whole(message)] * groups,
        ),
        out_shape=[
            jax.ShapeDtypeStruct((leaves, rank, ports), jnp.float32),
            jax.ShapeDtypeStruct((up_rows, ports), jnp.float32),
        ]
        + [jax.ShapeDtypeStruct(message, jnp.float32)] * groups,
        compiler_params=params(60 * MIB),
        cost_estimate=cost(10**9, 10**7),
        name="up_sweep",
    )(
        leaf_size, leaf_parent, slots, group_at, lane_at, charges, basis, transfer, mid_transfer, send_mid
    )


def spread_kernel(send, coef, out):
    leaves = coef.shape[0]

    @pl.loop(0, out.shape[0], unroll=8)
    def _(slot):
        out[slot] = coef[jnp.minimum(send[slot], leaves - 1)]


def spread(send_leaf, coef):
    vmem = pl.BlockSpec(memory_space=pltpu.VMEM)
    shape = (send_leaf.shape[0],) + coef.shape[1:]
    return pl.pallas_call(
        spread_kernel,
        in_specs=[pl.BlockSpec(memory_space=pltpu.SMEM), vmem],
        out_specs=vmem,
        out_shape=jax.ShapeDtypeStruct(shape, jnp.float32),
        compiler_params=params(60 * MIB),
        cost_estimate=cost(0, 4 * 10**6),
        name="spread",
    )(send_leaf, coef)


def select_kernel(sizes, group_at, lane_at, *refs):
    lines, per_cluster, up_rows, mids, rank, per_pair, groups = sizes
    received, messages = refs[:lines], refs[lines : lines + groups]
    payloads, tables, sem, table_sem = refs[lines + groups :]
    group, lane = group_at[0], lane_at[0]
    table_rows = up_rows - (mids + 1) * rank
    ports = payloads.shape[2]
    copies = []
    for line, ref in enumerate(received):
        table = ref.at[pl.ds((mids + 1) * rank, table_rows), :]
        copies.append(pltpu.make_async_copy(table, tables.at[line], table_sem.at[line]))
        copies.append(pltpu.make_async_copy(ref, payloads.at[line], sem.at[line]))
    for copy in copies:
        copy.start()
    for copy in copies:
        copy.wait()
    for d, message in enumerate(messages):
        for side in range(2):
            receiver = (group ^ d) * per_cluster + (lane ^ side)

            @pl.loop(0, lines, unroll=min(lines, 4))
            def _(line):
                for j in range(per_pair):
                    entry = receiver * per_pair + j
                    listed = tables[line, lax.div(entry, ports), lax.rem(entry, ports)]
                    block = jnp.clip(listed.astype(jnp.int32), 0, mids - 1)
                    target = (1 - side) * (per_pair + 1) * lines + line * per_pair + j
                    message[target] = payloads[line, pl.ds(pl.multiple_of(block * rank, 8), rank), :]

        for line in range(lines):
            message[lines * per_pair + line] = payloads[line, mids * rank : (mids + 1) * rank, :]


def select(sizes, group_at, lane_at, received):
    lines, per_cluster, up_rows, mids, rank, per_pair, groups = sizes
    ports = received[0].shape[1]
    table_rows = up_rows - (mids + 1) * rank
    payloads = (lines, up_rows, ports)
    shape = jax.ShapeDtypeStruct((lines * (2 * per_pair + 1), rank, ports), jnp.float32)
    return pl.pallas_call(
        functools.partial(select_kernel, sizes),
        in_specs=[pl.BlockSpec(memory_space=pltpu.SMEM)] * 2
        + [pl.BlockSpec(memory_space=pl.ANY)] * len(received),
        out_specs=[pl.BlockSpec(memory_space=pltpu.VMEM)] * groups,
        out_shape=[shape] * groups,
        scratch_shapes=[
            pltpu.VMEM(payloads, jnp.float32),
            pltpu.SMEM((lines, table_rows, ports), jnp.float32),
            pltpu.SemaphoreType.DMA((lines,)),
            pltpu.SemaphoreType.DMA((lines,)),
        ],
        compiler_params=params(60 * MIB),
        cost_estimate=cost(0, 4 * 10**6),
        name="select",
    )(group_at, lane_at, *received)


def prepare_kernel(after, coupling, basis, transfer, mid_coupling, mid_transfer, *out):
    wide, basis_t, transfer_t, mid_wide, mid_transfer_t = out
    for g in range(coupling.shape[0]):
        wide[g] = rows_of(coupling[g])
        basis_t[g] = rows_of(basis[g]).T
        transfer_t[g] = rows_of(transfer[g]).T
    for g in range(mid_coupling.shape[0]):
        mid_wide[g] = rows_of(mid_coupling[g])
        mid_transfer_t[g] = rows_of(mid_transfer[g]).T


def prepare(after, coupling, basis, transfer, mid_coupling, mid_transfer):
    leaves, rank, width = coupling.shape
    points = basis.shape[2]
    mids, _, mid_width = mid_coupling.shape
    steps = mids
    group = leaves // steps
    shapes = [
        (leaves, 2 * rank, width),
        (leaves, points, 2 * rank),
        (leaves, rank, 2 * rank),
        (mids, 2 * rank, mid_width),
        (mids, rank, 2 * rank),
    ]
    return pl.pallas_call(
        prepare_kernel,
        grid=(steps,),
        in_specs=[
            pl.BlockSpec(memory_space=pl.ANY),
            first(group, rank, width),
            first(group, rank, points),
            first(group, rank, rank),
            first(1, rank, mid_width),
            first(1, rank, rank),
        ],
        out_specs=[first(s[0] // steps, *s[1:]) for s in shapes],
        out_shape=[jax.ShapeDtypeStruct(s, jnp.bfloat16) for s in shapes],
        compiler_params=params(60 * MIB),
        cost_estimate=cost(0, 3 * 10**7),
        name="prepare",
    )(after, coupling, basis, transfer, mid_coupling, mid_transfer)


def tail_kernel(
    sizes, parent, pair, position, tops, size, pair_leaf, *refs
):
    bounds, per_pair, groups, chunk, group = sizes
    lines, count = bounds[-1], (len(bounds) - 1) * groups
    messages = refs[: 2 * count]
    (arrived, mid_wide, mid_transfer, transfer, top_coupling, wide, basis, out) = refs[2 * count : 2 * count + 8]
    scratch = refs[2 * count + 8 :]
    held_messages, scratch = scratch[: 2 * count], scratch[2 * count :]
    (
        arrived_held, mid_wide_held, mid_transfer_held, transfer_held, top_held, wide_held, basis_held,
        parts, top_parts, leaf_parts, near_top, down, back, out_held,
        message_sem, arrived_sem, mid_sem, small_sem, wide_sem, basis_sem, out_sem,
    ) = scratch
    mids, leaves = mid_wide.shape[0], wide.shape[0]
    rank, ports = back.shape[1:]
    slots, top_count = parts.shape[0] - 1, top_parts.shape[0] - 1
    points = basis.shape[1]

    def fetch_message(index):
        held = held_messages[index]
        start = 0 if index >= count else messages[index].shape[0] - held.shape[0]
        source = messages[index].at[pl.ds(start, held.shape[0])]
        return pltpu.make_async_copy(source, held, message_sem.at[index])

    def fetch_arrived(index):
        source = arrived.at[pl.ds(index * chunk, chunk)]
        return pltpu.make_async_copy(source, arrived_held.at[index % 2], arrived_sem.at[index % 2])

    def fetch_mid(c):
        return pltpu.make_async_copy(mid_wide.at[c], mid_wide_held.at[c], mid_sem.at[c])

    def fetch_leaves(index):
        some = pl.ds(index * group, group)
        return (
            pltpu.make_async_copy(wide.at[some], wide_held.at[some], wide_sem.at[index]),
            pltpu.make_async_copy(basis.at[some], basis_held.at[some], basis_sem.at[index]),
        )

    small = (
        pltpu.make_async_copy(top_coupling.at[position[0]], top_held, small_sem.at[0]),
        pltpu.make_async_copy(mid_transfer, mid_transfer_held, small_sem.at[1]),
        pltpu.make_async_copy(transfer, transfer_held, small_sem.at[2]),
    )
    chunks = slots // chunk
    for index in range(min(2, chunks)):
        fetch_arrived(index).start()
    for index in range(2 * count):
        fetch_message(index).start()
    for copy in small:
        copy.start()
    for c in range(mids):
        fetch_mid(c).start()
    for index in range(leaves // group):
        for copy in fetch_leaves(index):
            copy.start()

    leaf_parts[slots] = jnp.zeros(leaf_parts.shape[1:], jnp.bfloat16)
    parts[slots] = jnp.zeros(parts.shape[1:], jnp.bfloat16)
    top_parts[top_count] = jnp.zeros(top_parts.shape[1:], jnp.bfloat16)
    for index in range(chunks):
        fetch_arrived(index).wait()

        @pl.loop(0, chunk, unroll=8)
        def _(slot):
            leaf_parts[index * chunk + slot] = lanes_of(arrived_held[index % 2, slot])

        if index + 2 < chunks:
            fetch_arrived(index + 2).start()

    for index in range(2 * count):
        side, message = divmod(index, count)
        batch, d = divmod(message, groups)
        lines_held = bounds[batch + 1] - bounds[batch]
        piece = lines_held * per_pair
        base = (d * 2 + side) * lines + bounds[batch]
        held = held_messages[index]
        first_slot, first_top = (lines_held, 0) if side == 0 else (0, piece)
        fetch_message(index).wait()

        @pl.loop(0, piece, unroll=min(piece, 6))
        def _(slot):
            parts[base * per_pair + slot] = lanes_of(held[first_slot + slot])

        for line in range(lines_held):
            top_parts[base + line] = lanes_of(held[first_top + line])

    for copy in small:
        copy.wait()
    stacked = jnp.concatenate([top_parts[tops[k]] for k in range(tops.shape[0])], axis=0)
    near_top[...] = fold(dot(rows_of(top_held[...]), stacked))
    for c in range(mids):
        fetch_mid(c).wait()

    @pl.loop(0, mids, step=4)
    def _(start):
        near = []
        for g in range(4):
            c = start + g
            stacked = jnp.concatenate([parts[pair[c, k]] for k in range(pair.shape[1])], axis=0)
            value = fold(dot(mid_wide_held[c], stacked))
            near.append(value + deep_dot(mid_transfer_held[c], near_top[...]))
        for g in range(4):
            down[start + g] = near[g]

    @pl.loop(0, leaves, step=8)
    def _(start):
        terms = [deep_dot(transfer_held[start + g], down[parent[start + g]]) for g in range(8)]
        for g in range(8):
            back[start + g] = terms[g]

    point = lax.broadcasted_iota(jnp.int32, (points, ports), 0)

    def send(index):
        rows = group * points
        target = out.at[pl.ds(pl.multiple_of(index * rows, rows), rows), :]
        return pltpu.make_async_copy(out_held.at[index % 2], target, out_sem.at[index % 2])

    for index in range(leaves // group):
        for copy in fetch_leaves(index):
            copy.wait()
        values = []
        for g in range(group):
            leaf = index * group + g
            stacked = jnp.concatenate(
                [leaf_parts[pair_leaf[leaf, k]] for k in range(pair_leaf.shape[1])], axis=0
            )
            values.append(fold(dot(wide_held[leaf], stacked)) + back[leaf])
        if index >= 2:
            send(index - 2).wait()
        for g in range(group):
            far = deep_dot(basis_held[index * group + g], values[g])
            far = jnp.where(point < size[index * group + g], far, 0.0)
            out_held[index % 2, g * points : (g + 1) * points, :] = far
        send(index).start()
    for index in range(max(0, leaves // group - 2), leaves // group):
        send(index).wait()


def tail(
    bounds, per_pair, groups, parent, pair, position, tops, size, pair_leaf, near_side, far_side, arrived,
    mid_wide, mid_transfer, transfer, top_coupling, wide, basis
):
    mids, _, mid_width = mid_wide.shape
    leaves, points, _ = basis.shape
    slots, rank, ports = arrived.shape
    owners = slots // per_pair
    group, chunk = 4, min(slots, 32)
    held = []
    for message in range(len(near_side)):
        batch = message // groups
        held.append((bounds[batch + 1] - bounds[batch]) * (per_pair + 1))
    full, half = jnp.float32, jnp.bfloat16
    scratch = [((h, rank, ports), full) for h in held + held] + [
        ((2, chunk, rank, ports), full),
        (mid_wide.shape, half),
        (mid_transfer.shape, half),
        (transfer.shape, half),
        (top_coupling.shape[1:], full),
        (wide.shape, half),
        (basis.shape, half),
        ((slots + 1, rank, 2 * ports), half),
        ((owners + 1, rank, 2 * ports), half),
        ((slots + 1, rank, 2 * ports), half),
        ((rank, ports), full),
        ((mids, rank, ports), full),
        ((leaves, rank, ports), full),
        ((2, group * points, ports), full),
    ]
    semaphores = [2 * len(near_side), 2, mids, 3, leaves // group, leaves // group, 2]
    scalars = (parent, pair, position, tops, size, pair_leaf)
    arrays = (*near_side, *far_side, arrived, mid_wide, mid_transfer, transfer, top_coupling, wide, basis)
    return pl.pallas_call(
        functools.partial(tail_kernel, (bounds, per_pair, groups, chunk, group)),
        in_specs=[pl.BlockSpec(memory_space=pltpu.SMEM)] * len(scalars)
        + [pl.BlockSpec(memory_space=pl.ANY)] * len(arrays),
        out_specs=pl.BlockSpec(memory_space=pl.ANY),
        out_shape=jax.ShapeDtypeStruct((leaves * points, ports), full),
        scratch_shapes=[pltpu.VMEM(shape, dtype) for shape, dtype in scratch]
        + [pltpu.SemaphoreType.DMA((n,)) for n in semaphores],
        compiler_params=params(60 * MIB),
        cost_estimate=cost(6 * 10**9, 2 * 10**7),
        name="tail",
    )(*scalars, *arrays)


def body(
    charges, leaf_size, leaf_basis, leaf_transfer, mid_transfer, leaf_parent, send_leaf, pair_leaf,
    leaf_coupling, send_mid, pair_mid, mid_coupling, top_pairs, top_coupling,
):
    rank = leaf_basis.shape[1]
    ports = charges.shape[1]
    mids = mid_transfer.shape[0]
    slots = send_mid.shape[0]
    groups, per_cluster = lax.axis_size("group"), lax.axis_size("cluster")
    owners = groups * per_cluster
    lines = per_cluster // 2
    per_pair = slots // owners
    group, lane = lax.axis_index("group"), lax.axis_index("cluster")

    group_at, lane_at = group.astype(jnp.int32)[None], lane.astype(jnp.int32)[None]
    coef, lifted, *own_messages = up_sweep(
        (per_cluster, per_pair), groups, group_at, lane_at, charges, leaf_size, leaf_basis,
        leaf_transfer, mid_transfer, leaf_parent, send_mid,
    )
    up_rows = lifted.shape[0]
    outgoing = spread(send_leaf, coef)

    received = [lifted]
    for d in range(1, lines):
        received.append(
            lax.ppermute(lifted, "cluster", [(c, c ^ (2 * d)) for c in range(per_cluster)])
        )
    wide, basis_t, transfer_t, mid_wide, mid_transfer_t = prepare(
        lifted, leaf_coupling, leaf_basis, leaf_transfer, mid_coupling, mid_transfer
    )

    bounds = (0, 1, lines)
    near_side, far_side = [], []
    for low, high in zip(bounds[:-1], bounds[1:]):
        held = high - low
        sizes = (held, per_cluster, up_rows, mids, rank, per_pair, groups)
        messages = own_messages if low == 0 else select(sizes, group_at, lane_at, received[low:high])
        moved = [messages[0]]
        for d in range(1, groups):
            moved.append(lax.ppermute(messages[d], "group", [(g, g ^ d) for g in range(groups)]))
        if low == 0:
            outgoing, moved, received[1:] = lax.optimization_barrier((outgoing, moved, received[1:]))
            arrived = lax.all_to_all(outgoing, AXES, split_axis=0, concat_axis=0, tiled=True)
        else:
            moved, mid_wide = lax.optimization_barrier((moved, mid_wide))
        near_side += moved
        swap = [(c, c ^ 1) for c in range(per_cluster)]
        far_side += [lax.ppermute(m, "cluster", swap) for m in moved]

    def spot_of(sender):
        at_group, at_lane = sender // per_cluster, sender % per_cluster
        line = (at_lane // 2) ^ (lane // 2)
        return ((at_group ^ group) * 2 + ((at_lane ^ lane) & 1)) * lines + line

    spot = spot_of(pair_mid // per_pair) * per_pair + pair_mid % per_pair
    spot = jnp.where((pair_mid >= 0) & (pair_mid < slots), spot, slots)
    wanted = lax.dynamic_slice_in_dim(top_pairs, lane, 1, 0)[0]
    tops = jnp.where((wanted >= 0) & (wanted < owners), spot_of(wanted), owners)
    return tail(
        bounds, per_pair, groups, leaf_parent, spot, lane_at, tops, leaf_size, pair_leaf, near_side,
        far_side, arrived, mid_wide, mid_transfer_t, transfer_t, top_coupling, wide, basis_t,
    )


def solution(mesh):
    both = P(AXES)
    in_specs = (
        P(AXES, None),
        both,
        P(AXES, None, None),
        P(AXES, None, None),
        P(AXES, None, None),
        both,
        both,
        P(AXES, None),
        P(AXES, None, None),
        both,
        P(AXES, None),
        P(AXES, None, None),
        P("group", None),
        P("group", None, None),
    )
    return jax.shard_map(
        body, mesh=mesh, in_specs=in_specs, out_specs=P(AXES, None), check_vma=False
    )
```

profile of v0, /device:TPU:0, one launch (start us, length us, event | category | flops | bytes accessed | tf_op | source)
XLA Modules:
  0.0 112.9 jit_solution(4286560808012655690)
XLA Ops:
  0.0 7.4 %up_sweep.1 = (f32[32,64,128]{2,1,0:T(8,128)}, f32[584,128]{1,0:T(8,128)}, f32[5,64,128]{2,1,0:T(8,128)}, f32[5,64,128]{2,1,0:T(8,128)}, f32[5,64,128]{2,1,0:T(8,128)}, /*index=5*/f32[5,64,128]{2,1,0:T(8,128)}) custom-call(s32[32]{0:T(128)} %size.3, s32[32]{0:T(128)} %parent.3, s32[64]{0:T(128)} %slots.1, s32[1]{0:T(128)} %bitcast.1.group_at, ...), custom_call_target="tpu_custom_call" | custom-call | flops 1000000000 | bytes 10000000 | tf_op jit(solution)/shard_map/up_sweep/pallas_call | solution.py:119
  7.4 3.0 %collective-permute-start = (f32[5,64,128]{2,1,0:T(8,128)}, f32[5,64,128]{2,1,0:T(8,128)S(1)}, u32[]{:S(2)}, u32[]{:S(2)}) collective-permute-start(f32[5,64,128]{2,1,0:T(8,128)} %get-tuple-element.35), channel_id=1, source_target_pairs={{0,8},{8,0},{16,24},{24,16},{1,9},{9,1},{17,25},{25,17},{2,10},{10... | collective-permute-start | bytes 491528 | tf_op jit(solution)/shard_map/ppermute | solution.py:493
  10.4 3.6 %collective-permute-start.5 = (f32[584,128]{1,0:T(8,128)}, f32[584,128]{1,0:T(8,128)S(1)}, u32[]{:S(2)}, u32[]{:S(2)}) collective-permute-start(f32[584,128]{1,0:T(8,128)} %get-tuple-element.38.after), channel_id=1, source_target_pairs={{0,6},{1,7},{2,4},{3,5},{4,2},{5,3},{6,0},{7,1},{8,14},{9,15},{10,... | collective-permute-start | bytes 897032 | tf_op jit(solution)/shard_map/ppermute | solution.py:479
  14.0 0.0 collective-permute-start.4
  14.0 0.8 collective-permute-start.3
  14.8 1.5 %collective-permute-start.1 = (f32[5,64,128]{2,1,0:T(8,128)}, f32[5,64,128]{2,1,0:T(8,128)S(1)}, u32[]{:S(2)}, u32[]{:S(2)}) collective-permute-start(f32[5,64,128]{2,1,0:T(8,128)} %get-tuple-element.36), channel_id=1, source_target_pairs={{0,16},{8,24},{16,0},{24,8},{1,17},{9,25},{17,1},{25,9},{2,18},{10... | collective-permute-start | bytes 491528 | tf_op jit(solution)/shard_map/ppermute | solution.py:493
  16.3 0.0 collective-permute-done.refs_1_
  16.3 1.2 %collective-permute-start.2 = (f32[5,64,128]{2,1,0:T(8,128)}, f32[5,64,128]{2,1,0:T(8,128)S(1)}, u32[]{:S(2)}, u32[]{:S(2)}) collective-permute-start(f32[5,64,128]{2,1,0:T(8,128)} %get-tuple-element.37), channel_id=1, source_target_pairs={{0,24},{8,16},{16,8},{24,0},{1,25},{9,17},{17,9},{25,1},{2,26},{10... | collective-permute-start | bytes 491528 | tf_op jit(solution)/shard_map/ppermute | solution.py:493
  17.5 2.7 %spread.1 = f32[64,64,128]{2,1,0:T(8,128)} custom-call(s32[64]{0:T(128)} %send.1, f32[32,64,128]{2,1,0:T(8,128)} %get-tuple-element.33.coef), custom_call_target="tpu_custom_call" | custom-call | bytes 4000000 | tf_op jit(solution)/shard_map/spread/pallas_call | solution.py:157
  20.2 3.5 %collective-permute-done.1.refs_2_ = f32[5,64,128]{2,1,0:T(8,128)S(1)} collective-permute-done((f32[5,64,128]{2,1,0:T(8,128)}, f32[5,64,128]{2,1,0:T(8,128)S(1)}, u32[]{:S(2)}, u32[]{:S(2)}) %collective-permute-start.1) | collective-permute-done | bytes 163872 | tf_op jit(solution)/shard_map/ppermute | solution.py:493
  23.8 0.0 collective-permute-done.2.refs_3_
  23.8 0.0 collective-permute-done.5.refs_2_
  23.8 15.6 %collective-permute-done.4.refs_1_ = f32[584,128]{1,0:T(8,128)S(1)} collective-permute-done((f32[584,128]{1,0:T(8,128)}, f32[584,128]{1,0:T(8,128)S(1)}, u32[]{:S(2)}, u32[]{:S(2)}) %collective-permute-start.4) | collective-permute-done | bytes 299040 | tf_op jit(solution)/shard_map/ppermute | solution.py:479
  39.4 0.0 collective-permute-done.3.refs_0_
  39.4 3.8 %all-to-all-start = ((f32[64,64,128]{2,1,0:T(8,128)}), f32[64,64,128]{2,1,0:T(8,128)S(1)}, u32[]{:S(2)}, u32[]{:S(2)}) async-start(f32[64,64,128]{2,1,0:T(8,128)} %spread.1), calls=%async_computation | async-start | bytes 4194304 | tf_op jit(solution)/shard_map/all_to_all | solution.py:496
  43.2 2.7 %select.31 = (f32[15,64,128]{2,1,0:T(8,128)}, f32[15,64,128]{2,1,0:T(8,128)}, f32[15,64,128]{2,1,0:T(8,128)}, f32[15,64,128]{2,1,0:T(8,128)}) custom-call(s32[1]{0:T(128)} %bitcast.1.group_at, s32[1]{0:T(128)} %bitcast.lane_at.position, f32[584,128]{1,0:T(8,128)} %copy-done.6, f32[584,128]{1,0:T(8,128)} %copy-done.5, f32[584,128]{1,0:T(8,128)} %copy-done.4), custom_call_target="tpu_custom_call" | custom-call | bytes 4000000 | tf_op jit(solution)/shard_map/select/pallas_call | solution.py:207
  46.0 1.8 %collective-permute-start.6 = (f32[15,64,128]{2,1,0:T(8,128)}, f32[15,64,128]{2,1,0:T(8,128)S(1)}, u32[]{:S(2)}, u32[]{:S(2)}) collective-permute-start(f32[15,64,128]{2,1,0:T(8,128)} %get-tuple-element.47), channel_id=1, source_target_pairs={{0,8},{8,0},{16,24},{24,16},{1,9},{9,1},{17,25},{25,17},{2,10},{10... | collective-permute-start | bytes 1474568 | tf_op jit(solution)/shard_map/ppermute | solution.py:493
  47.8 1.5 %collective-permute-start.7 = (f32[15,64,128]{2,1,0:T(8,128)}, f32[15,64,128]{2,1,0:T(8,128)}, u32[]{:S(2)}, u32[]{:S(2)}) collective-permute-start(f32[15,64,128]{2,1,0:T(8,128)} %get-tuple-element.48), channel_id=1, source_target_pairs={{0,16},{8,24},{16,0},{24,8},{1,17},{9,25},{17,1},{25,9},{2,18},{10... | collective-permute-start | bytes 1474568 | tf_op jit(solution)/shard_map/ppermute | solution.py:493
  49.3 0.3 collective-permute-start.8
  49.5 0.0 collective-permute-start.9
  49.5 0.5 collective-permute-start.10
  50.0 11.9 %prepare.1 = (bf16[32,128,768]{2,1,0:T(8,128)(2,1)}, bf16[32,256,128]{2,1,0:T(8,128)(2,1)}, bf16[32,64,128]{2,1,0:T(8,128)(2,1)}, bf16[8,128,2048]{2,1,0:T(8,128)(2,1)}, bf16[8,64,128]{2,1,0:T(8,128)(2,1)}) custom-call(f32[584,128]{1,0:T(8,128)} %get-tuple-element.38.after, f32[32,64,768]{2,1,0:T(8,128)} %coupling.1, f32[32,64,256]{2,1,0:T(8,128)} %basis.3, ...), custom_call_target="tpu_custom_call" | custom-call | bytes 30000000 | tf_op jit(solution)/shard_map/prepare/pallas_call | solution.py:249
  61.9 11.8 %collective-permute-done.6.refs_5_ = f32[15,64,128]{2,1,0:T(8,128)S(1)} collective-permute-done((f32[15,64,128]{2,1,0:T(8,128)}, f32[15,64,128]{2,1,0:T(8,128)S(1)}, u32[]{:S(2)}, u32[]{:S(2)}) %collective-permute-start.6) | collective-permute-done | bytes 491552 | tf_op jit(solution)/shard_map/ppermute | solution.py:493
  73.7 3.1 %collective-permute-done.7.refs_6_ = f32[15,64,128]{2,1,0:T(8,128)} collective-permute-done((f32[15,64,128]{2,1,0:T(8,128)}, f32[15,64,128]{2,1,0:T(8,128)}, u32[]{:S(2)}, u32[]{:S(2)}) %collective-permute-start.7) | collective-permute-done | bytes 491552 | tf_op jit(solution)/shard_map/ppermute | solution.py:493
  76.8 12.2 %collective-permute-done.8.refs_7_ = f32[15,64,128]{2,1,0:T(8,128)} collective-permute-done((f32[15,64,128]{2,1,0:T(8,128)}, f32[15,64,128]{2,1,0:T(8,128)}, u32[]{:S(2)}, u32[]{:S(2)}) %collective-permute-start.8) | collective-permute-done | bytes 491552 | tf_op jit(solution)/shard_map/ppermute | solution.py:493
  89.0 0.0 collective-permute-start.13
  89.0 0.5 collective-permute-start.14
  89.5 0.0 collective-permute-start.15
  89.5 0.0 collective-permute-done.9.refs_8_
  89.5 0.7 copy-done.11
  90.2 0.5 collective-permute-start.16
  90.7 0.7 copy.15.pair_leaf
  91.4 0.2 dynamic-slice_reduce_fusion
  91.6 0.0 collective-permute-done.10.refs_9_
  91.6 0.1 collective-permute-start.11
  91.7 0.6 fusion.7.pair
  92.3 1.1 %collective-permute-done.11.refs_10_ = f32[5,64,128]{2,1,0:T(8,128)S(1)} collective-permute-done((f32[5,64,128]{2,1,0:T(8,128)}, f32[5,64,128]{2,1,0:T(8,128)S(1)}, u32[]{:S(2)}, u32[]{:S(2)}) %collective-permute-start.11) | collective-permute-done | bytes 163872 | tf_op jit(solution)/shard_map/ppermute | solution.py:501
  93.4 0.1 collective-permute-start.12
  93.6 0.6 and_select_fusion.3.tops
  94.2 0.9 collective-permute-done.12.refs_11_
  95.0 0.0 collective-permute-done.13.refs_12_
  95.0 0.0 collective-permute-done.14.refs_13_
  95.0 0.0 collective-permute-done.15.refs_14_
  95.1 0.0 collective-permute-done.16.refs_15_
  95.1 0.0 all-to-all-done.refs_16_
  95.1 0.6 copy-done.13
  95.7 0.7 copy-done.1
  96.4 16.5 %tail.1 = f32[8192,128]{1,0:T(8,128)} custom-call(s32[32]{0:T(128)} %parent.3, s32[8,32]{1,0:T(8,128)} %fusion.7.pair, s32[1]{0:T(128)} %bitcast.lane_at.position, s32[4]{0:T(128)} %and_select_fusion.3.tops, s32[32]{0:T(128)} %size.3, s32[32,12]{1,0:T(8,128)} %copy.15.pair_leaf, f32[5,64,128]{2,1,0:T(8,128)} %get-tuple-element.39.refs_0_, ...), custom_call_target="tpu_custom_call" | custom-call | flops 6000000000 | bytes 20000000 | tf_op jit(solution)/shard_map/tail/pallas_call | solution.py:440
  (29 shorter events, 0.1 us)
Async XLA Ops:
  0.0 91.4 %copy-start = (s32[8,4]{0,1:T(4,128)S(1)}, s32[8,4]{0,1:T(4,128)}, u32[]{:S(2)}) copy-start(s32[8,4]{0,1:T(4,128)} %param.26) | copy-start | bytes 388
  7.4 42.2 %copy-start.7 = (f32[5,64,128]{2,1,0:T(8,128)S(1)}, f32[5,64,128]{2,1,0:T(8,128)}, u32[]{:S(2)}) copy-start(f32[5,64,128]{2,1,0:T(8,128)} %get-tuple-element.39.refs_0_) | copy-start | bytes 491524
  7.4 8.9 %collective-permute-start = (f32[5,64,128]{2,1,0:T(8,128)}, f32[5,64,128]{2,1,0:T(8,128)S(1)}, u32[]{:S(2)}, u32[]{:S(2)}) collective-permute-start(f32[5,64,128]{2,1,0:T(8,128)} %get-tuple-element.35), channel_id=1, source_target_pairs={{0,8},{8,0},{16,24},{24,16},{1,9},{9,1},{17,25},{25,17},{2,10},{10... | collective-permute-start | bytes 491528 | tf_op jit(solution)/shard_map/ppermute | solution.py:493
  10.4 13.4 %collective-permute-start.5 = (f32[584,128]{1,0:T(8,128)}, f32[584,128]{1,0:T(8,128)S(1)}, u32[]{:S(2)}, u32[]{:S(2)}) collective-permute-start(f32[584,128]{1,0:T(8,128)} %get-tuple-element.38.after), channel_id=1, source_target_pairs={{0,6},{1,7},{2,4},{3,5},{4,2},{5,3},{6,0},{7,1},{8,14},{9,15},{10,... | collective-permute-start | bytes 897032 | tf_op jit(solution)/shard_map/ppermute | solution.py:479
  14.0 25.4 %collective-permute-start.4 = (f32[584,128]{1,0:T(8,128)}, f32[584,128]{1,0:T(8,128)S(1)}, u32[]{:S(2)}, u32[]{:S(2)}) collective-permute-start(f32[584,128]{1,0:T(8,128)} %get-tuple-element.38.after), channel_id=1, source_target_pairs={{0,4},{1,5},{2,6},{3,7},{4,0},{5,1},{6,2},{7,3},{8,12},{9,13},{10,... | collective-permute-start | bytes 897032 | tf_op jit(solution)/shard_map/ppermute | solution.py:479
  14.0 25.4 %collective-permute-start.3 = (f32[584,128]{1,0:T(8,128)}, f32[584,128]{1,0:T(8,128)S(1)}, u32[]{:S(2)}, u32[]{:S(2)}) collective-permute-start(f32[584,128]{1,0:T(8,128)} %get-tuple-element.38.after), channel_id=1, source_target_pairs={{0,2},{1,3},{2,0},{3,1},{4,6},{5,7},{6,4},{7,5},{8,10},{9,11},{10,... | collective-permute-start | bytes 897032 | tf_op jit(solution)/shard_map/ppermute | solution.py:479
  14.8 9.0 %collective-permute-start.1 = (f32[5,64,128]{2,1,0:T(8,128)}, f32[5,64,128]{2,1,0:T(8,128)S(1)}, u32[]{:S(2)}, u32[]{:S(2)}) collective-permute-start(f32[5,64,128]{2,1,0:T(8,128)} %get-tuple-element.36), channel_id=1, source_target_pairs={{0,16},{8,24},{16,0},{24,8},{1,17},{9,25},{17,1},{25,9},{2,18},{10... | collective-permute-start | bytes 491528 | tf_op jit(solution)/shard_map/ppermute | solution.py:493
  16.3 45.6 %copy-start.8 = (f32[5,64,128]{2,1,0:T(8,128)}, f32[5,64,128]{2,1,0:T(8,128)S(1)}, u32[]{:S(2)}) copy-start(f32[5,64,128]{2,1,0:T(8,128)S(1)} %collective-permute-done.refs_1_) | copy-start | bytes 491524
  16.3 7.5 %collective-permute-start.2 = (f32[5,64,128]{2,1,0:T(8,128)}, f32[5,64,128]{2,1,0:T(8,128)S(1)}, u32[]{:S(2)}, u32[]{:S(2)}) collective-permute-start(f32[5,64,128]{2,1,0:T(8,128)} %get-tuple-element.37), channel_id=1, source_target_pairs={{0,24},{8,16},{16,8},{24,0},{1,25},{9,17},{17,9},{25,1},{2,26},{10... | collective-permute-start | bytes 491528 | tf_op jit(solution)/shard_map/ppermute | solution.py:493
  23.8 15.6 %copy-start.9 = (f32[5,64,128]{2,1,0:T(8,128)}, f32[5,64,128]{2,1,0:T(8,128)S(1)}, u32[]{:S(2)}) copy-start(f32[5,64,128]{2,1,0:T(8,128)S(1)} %collective-permute-done.1.refs_2_) | copy-start | bytes 491524
  23.8 15.6 %copy-start.10 = (f32[5,64,128]{2,1,0:T(8,128)}, f32[5,64,128]{2,1,0:T(8,128)S(1)}, u32[]{:S(2)}) copy-start(f32[5,64,128]{2,1,0:T(8,128)S(1)} %collective-permute-done.2.refs_3_) | copy-start | bytes 491524
  23.8 19.5 %copy-start.4 = (f32[584,128]{1,0:T(8,128)}, f32[584,128]{1,0:T(8,128)S(1)}, u32[]{:S(2)}) copy-start(f32[584,128]{1,0:T(8,128)S(1)} %collective-permute-done.5.refs_2_) | copy-start | bytes 897028
  39.4 3.8 %copy-start.5 = (f32[584,128]{1,0:T(8,128)}, f32[584,128]{1,0:T(8,128)S(1)}, u32[]{:S(2)}) copy-start(f32[584,128]{1,0:T(8,128)S(1)} %collective-permute-done.4.refs_1_) | copy-start | bytes 897028
  39.4 3.8 %copy-start.6 = (f32[584,128]{1,0:T(8,128)}, f32[584,128]{1,0:T(8,128)S(1)}, u32[]{:S(2)}) copy-start(f32[584,128]{1,0:T(8,128)S(1)} %collective-permute-done.3.refs_0_) | copy-start | bytes 897028
  39.4 55.6 %all-to-all-start = ((f32[64,64,128]{2,1,0:T(8,128)}), f32[64,64,128]{2,1,0:T(8,128)S(1)}, u32[]{:S(2)}, u32[]{:S(2)}) async-start(f32[64,64,128]{2,1,0:T(8,128)} %spread.1), calls=%async_computation | async-start | bytes 4194304 | tf_op jit(solution)/shard_map/all_to_all | solution.py:496
  46.0 27.8 %collective-permute-start.6 = (f32[15,64,128]{2,1,0:T(8,128)}, f32[15,64,128]{2,1,0:T(8,128)S(1)}, u32[]{:S(2)}, u32[]{:S(2)}) collective-permute-start(f32[15,64,128]{2,1,0:T(8,128)} %get-tuple-element.47), channel_id=1, source_target_pairs={{0,8},{8,0},{16,24},{24,16},{1,9},{9,1},{17,25},{25,17},{2,10},{10... | collective-permute-start | bytes 1474568 | tf_op jit(solution)/shard_map/ppermute | solution.py:493
  47.8 29.0 %collective-permute-start.7 = (f32[15,64,128]{2,1,0:T(8,128)}, f32[15,64,128]{2,1,0:T(8,128)}, u32[]{:S(2)}, u32[]{:S(2)}) collective-permute-start(f32[15,64,128]{2,1,0:T(8,128)} %get-tuple-element.48), channel_id=1, source_target_pairs={{0,16},{8,24},{16,0},{24,8},{1,17},{9,25},{17,1},{25,9},{2,18},{10... | collective-permute-start | bytes 1474568 | tf_op jit(solution)/shard_map/ppermute | solution.py:493
  49.3 39.8 %copy-start.2 = (f32[15,64,128]{2,1,0:T(8,128)S(1)}, f32[15,64,128]{2,1,0:T(8,128)}, u32[]{:S(2)}) copy-start(f32[15,64,128]{2,1,0:T(8,128)} %get-tuple-element.51.refs_4_) | copy-start | bytes 1474564
  49.3 41.4 %copy-start.14 = (s32[32,12]{0,1:T(8,128)S(1)}, s32[32,12]{0,1:T(8,128)}, u32[]{:S(2)}) copy-start(s32[32,12]{0,1:T(8,128)} %param.21) | copy-start | bytes 4612
  49.3 42.4 %copy-start.15 = (s32[8,32]{1,0:T(8,128)S(1)}, s32[8,32]{1,0:T(8,128)}, u32[]{:S(2)}) copy-start(s32[8,32]{1,0:T(8,128)} %param.24) | copy-start | bytes 3076
  49.3 39.7 %collective-permute-start.8 = (f32[15,64,128]{2,1,0:T(8,128)}, f32[15,64,128]{2,1,0:T(8,128)}, u32[]{:S(2)}, u32[]{:S(2)}) collective-permute-start(f32[15,64,128]{2,1,0:T(8,128)} %get-tuple-element.49), channel_id=1, source_target_pairs={{0,24},{8,16},{16,8},{24,0},{1,25},{9,17},{17,9},{25,1},{2,26},{10... | collective-permute-start | bytes 1474568 | tf_op jit(solution)/shard_map/ppermute | solution.py:493
  49.5 40.0 %collective-permute-start.9 = (f32[5,64,128]{2,1,0:T(8,128)S(1)}, f32[5,64,128]{2,1,0:T(8,128)S(1)}, u32[]{:S(2)}, u32[]{:S(2)}) collective-permute-start(f32[5,64,128]{2,1,0:T(8,128)S(1)} %copy-done.7), channel_id=1, source_target_pairs={{0,1},{1,0},{2,3},{3,2},{4,5},{5,4},{6,7},{7,6},{8,9},{9,8},{10,11... | collective-permute-start | bytes 491528 | tf_op jit(solution)/shard_map/ppermute | solution.py:501
  49.5 42.0 %collective-permute-start.10 = (f32[5,64,128]{2,1,0:T(8,128)S(1)}, f32[5,64,128]{2,1,0:T(8,128)}, u32[]{:S(2)}, u32[]{:S(2)}) collective-permute-start(f32[5,64,128]{2,1,0:T(8,128)S(1)} %collective-permute-done.refs_1_), channel_id=1, source_target_pairs={{0,1},{1,0},{2,3},{3,2},{4,5},{5,4},{6,7},{7,6},{8,9},{9,8},{10,11... | collective-permute-start | bytes 491528 | tf_op jit(solution)/shard_map/ppermute | solution.py:501
  73.7 21.3 %copy-start.3 = (f32[15,64,128]{2,1,0:T(8,128)}, f32[15,64,128]{2,1,0:T(8,128)S(1)}, u32[]{:S(2)}) copy-start(f32[15,64,128]{2,1,0:T(8,128)S(1)} %collective-permute-done.6.refs_5_) | copy-start | bytes 1474564
  89.0 6.0 %collective-permute-start.13 = (f32[15,64,128]{2,1,0:T(8,128)S(1)}, f32[15,64,128]{2,1,0:T(8,128)}, u32[]{:S(2)}, u32[]{:S(2)}) collective-permute-start(f32[15,64,128]{2,1,0:T(8,128)S(1)} %copy-done.2), channel_id=1, source_target_pairs={{0,1},{1,0},{2,3},{3,2},{4,5},{5,4},{6,7},{7,6},{8,9},{9,8},{10,11... | collective-permute-start | bytes 1474568 | tf_op jit(solution)/shard_map/ppermute | solution.py:501
  89.0 6.0 %collective-permute-start.14 = (f32[15,64,128]{2,1,0:T(8,128)S(1)}, f32[15,64,128]{2,1,0:T(8,128)}, u32[]{:S(2)}, u32[]{:S(2)}) collective-permute-start(f32[15,64,128]{2,1,0:T(8,128)S(1)} %collective-permute-done.6.refs_5_), channel_id=1, source_target_pairs={{0,1},{1,0},{2,3},{3,2},{4,5},{5,4},{6,7},{7,6},{8,9},{9,8},{10,11... | collective-permute-start | bytes 1474568 | tf_op jit(solution)/shard_map/ppermute | solution.py:501
  89.5 5.5 %collective-permute-start.15 = (f32[15,64,128]{2,1,0:T(8,128)}, f32[15,64,128]{2,1,0:T(8,128)}, u32[]{:S(2)}, u32[]{:S(2)}) collective-permute-start(f32[15,64,128]{2,1,0:T(8,128)} %collective-permute-done.7.refs_6_), channel_id=1, source_target_pairs={{0,1},{1,0},{2,3},{3,2},{4,5},{5,4},{6,7},{7,6},{8,9},{9,8},{10,11... | collective-permute-start | bytes 1474568 | tf_op jit(solution)/shard_map/ppermute | solution.py:501
  89.5 0.7 copy-start.11
  90.2 4.9 %collective-permute-start.16 = (f32[15,64,128]{2,1,0:T(8,128)}, f32[15,64,128]{2,1,0:T(8,128)}, u32[]{:S(2)}, u32[]{:S(2)}) collective-permute-start(f32[15,64,128]{2,1,0:T(8,128)} %collective-permute-done.8.refs_7_), channel_id=1, source_target_pairs={{0,1},{1,0},{2,3},{3,2},{4,5},{5,4},{6,7},{7,6},{8,9},{9,8},{10,11... | collective-permute-start | bytes 1474568 | tf_op jit(solution)/shard_map/ppermute | solution.py:501
  91.6 1.9 %collective-permute-start.11 = (f32[5,64,128]{2,1,0:T(8,128)}, f32[5,64,128]{2,1,0:T(8,128)S(1)}, u32[]{:S(2)}, u32[]{:S(2)}) collective-permute-start(f32[5,64,128]{2,1,0:T(8,128)} %copy-done.9), channel_id=1, source_target_pairs={{0,1},{1,0},{2,3},{3,2},{4,5},{5,4},{6,7},{7,6},{8,9},{9,8},{10,11... | collective-permute-start | bytes 491528 | tf_op jit(solution)/shard_map/ppermute | solution.py:501
  93.4 1.7 %copy-start.12 = (f32[5,64,128]{2,1,0:T(8,128)}, f32[5,64,128]{2,1,0:T(8,128)S(1)}, u32[]{:S(2)}) copy-start(f32[5,64,128]{2,1,0:T(8,128)S(1)} %collective-permute-done.11.refs_10_) | copy-start | bytes 491524
  93.4 1.6 %collective-permute-start.12 = (f32[5,64,128]{2,1,0:T(8,128)}, f32[5,64,128]{2,1,0:T(8,128)S(1)}, u32[]{:S(2)}, u32[]{:S(2)}) collective-permute-start(f32[5,64,128]{2,1,0:T(8,128)} %copy-done.10), channel_id=1, source_target_pairs={{0,1},{1,0},{2,3},{3,2},{4,5},{5,4},{6,7},{7,6},{8,9},{9,8},{10,11... | collective-permute-start | bytes 491528 | tf_op jit(solution)/shard_map/ppermute | solution.py:501
  95.0 0.7 copy-start.13
  95.1 1.3 %copy-start.1 = (f32[64,64,128]{2,1,0:T(8,128)}, f32[64,64,128]{2,1,0:T(8,128)S(1)}, u32[]{:S(2)}) copy-start(f32[64,64,128]{2,1,0:T(8,128)S(1)} %all-to-all-done.refs_16_) | copy-start | bytes 6291460
where the time goes:
time: 115 us; the launch traced here: 113 us
  waiting for transfers between devices  48.3 us (42%)
  Pallas kernels  41.2 us (36%)
  starting transfers between devices  19.2 us (17%)
  local copies, waits for them, and re-layouts  2.86 us (2%)
  other arithmetic  1.21 us (1%)
    ppermute x6, waiting for transfers between devices, body(): lax.ppermute(messages[d], 'group', [(g, g ^ d) for g in range(groups)])  30.6 us
    pallas_call x1, Pallas kernels, tail(): pl.pallas_call(functools.partial(tail_kernel, (bounds, per_pair, groups,...  16.5 us
    ppermute x3, waiting for transfers between devices, body(): lax.ppermute(lifted, 'cluster', [(c, c ^ 2 * d) for c in range(per_cluste...  15.6 us
    pallas_call x1, Pallas kernels, prepare(): pl.pallas_call(prepare_kernel, grid=(steps,), in_specs=[pl.BlockSpec(memo...  11.9 us
    ppermute x6, starting transfers between devices, body(): lax.ppermute(messages[d], 'group', [(g, g ^ d) for g in range(groups)])  9.28 us
    pallas_call x1, Pallas kernels, up_sweep(): pl.pallas_call(functools.partial(up_kernel, sizes), grid_spec=pltpu.Prefe...  7.36 us
    ppermute x3, starting transfers between devices, body(): lax.ppermute(lifted, 'cluster', [(c, c ^ 2 * d) for c in range(per_cluste...  4.39 us
    all_to_all x1, starting transfers between devices, body(): lax.all_to_all(outgoing, AXES, split_axis=0, concat_axis=0, tiled=True)  3.79 us
  transfers between devices with their start and end apart: 18, of which 7 were waited for; matrix products, arithmetic and copies ran while one was open for 2% of the time, Pallas kernels for 15%

commit v1 on v0

--- a/solution.py
+++ b/solution.py
@@ -222,15 +222,12 @@
     )(group_at, lane_at, *received)
 
 
-def prepare_kernel(after, coupling, basis, transfer, mid_coupling, mid_transfer, *out):
-    wide, basis_t, transfer_t, mid_wide, mid_transfer_t = out
+def prepare_kernel(after, coupling, basis, transfer, mid_coupling, mid_transfer, wide, basis_t, mid_wide):
     for g in range(coupling.shape[0]):
-        wide[g] = rows_of(coupling[g])
+        wide[g] = rows_of(jnp.concatenate([coupling[g], transfer[g].T], axis=1))
         basis_t[g] = rows_of(basis[g]).T
-        transfer_t[g] = rows_of(transfer[g]).T
     for g in range(mid_coupling.shape[0]):
-        mid_wide[g] = rows_of(mid_coupling[g])
-        mid_transfer_t[g] = rows_of(mid_transfer[g]).T
+        mid_wide[g] = rows_of(jnp.concatenate([mid_coupling[g], mid_transfer[g].T], axis=1))
 
 
 def prepare(after, coupling, basis, transfer, mid_coupling, mid_transfer):
@@ -240,11 +237,9 @@
     steps = mids
     group = leaves // steps
     shapes = [
-        (leaves, 2 * rank, width),
+        (leaves, 2 * rank, width + rank),
         (leaves, points, 2 * rank),
-        (leaves, rank, 2 * rank),
-        (mids, 2 * rank, mid_width),
-        (mids, rank, 2 * rank),
+        (mids, 2 * rank, mid_width + rank),
     ]
     return pl.pallas_call(
         prepare_kernel,
@@ -265,24 +260,21 @@
     )(after, coupling, basis, transfer, mid_coupling, mid_transfer)
 
 
-def tail_kernel(
-    sizes, parent, pair, position, tops, size, pair_leaf, *refs
-):
-    bounds, per_pair, groups, chunk, group = sizes
+def tail_kernel(sizes, parent, pair, position, tops, size, pair_leaf, *refs):
+    bounds, per_pair, groups, chunk, group, ahead = sizes
     lines, count = bounds[-1], (len(bounds) - 1) * groups
     messages = refs[: 2 * count]
-    (arrived, mid_wide, mid_transfer, transfer, top_coupling, wide, basis, out) = refs[2 * count : 2 * count + 8]
-    scratch = refs[2 * count + 8 :]
+    arrived, mid_wide, top_coupling, wide, basis, out = refs[2 * count : 2 * count + 6]
+    scratch = refs[2 * count + 6 :]
     held_messages, scratch = scratch[: 2 * count], scratch[2 * count :]
     (
-        arrived_held, mid_wide_held, mid_transfer_held, transfer_held, top_held, wide_held, basis_held,
-        parts, top_parts, leaf_parts, near_top, down, back, out_held,
-        message_sem, arrived_sem, mid_sem, small_sem, wide_sem, basis_sem, out_sem,
+        arrived_held, mid_wide_held, top_held, wide_held, basis_held, parts, top_parts, leaf_parts, out_held,
+        message_sem, arrived_sem, mid_sem, top_sem, wide_sem, basis_sem, out_sem,
     ) = scratch
-    mids, leaves = mid_wide.shape[0], wide.shape[0]
-    rank, ports = back.shape[1:]
-    slots, top_count = parts.shape[0] - 1, top_parts.shape[0] - 1
-    points = basis.shape[1]
+    mids, leaves, points = mid_wide.shape[0], wide.shape[0], basis.shape[1]
+    slots, top_count = arrived.shape[0], top_parts.shape[0] - 1
+    ports = out.shape[1]
+    steps, chunks = leaves // group, slots // chunk
 
     def fetch_message(index):
         held = held_messages[index]
@@ -304,29 +296,21 @@
             pltpu.make_async_copy(basis.at[some], basis_held.at[some], basis_sem.at[index]),
         )
 
-    small = (
-        pltpu.make_async_copy(top_coupling.at[position[0]], top_held, small_sem.at[0]),
-        pltpu.make_async_copy(mid_transfer, mid_transfer_held, small_sem.at[1]),
-        pltpu.make_async_copy(transfer, transfer_held, small_sem.at[2]),
-    )
-    chunks = slots // chunk
+    fetch_top = pltpu.make_async_copy(top_coupling.at[position[0]], top_held, top_sem)
     for index in range(min(2, chunks)):
         fetch_arrived(index).start()
     for index in range(2 * count):
         fetch_message(index).start()
-    for copy in small:
-        copy.start()
-    for c in range(mids):
-        fetch_mid(c).start()
-    for index in range(leaves // group):
-        for copy in fetch_leaves(index):
-            copy.start()
+    fetch_top.start()
 
     leaf_parts[slots] = jnp.zeros(leaf_parts.shape[1:], jnp.bfloat16)
     parts[slots] = jnp.zeros(parts.shape[1:], jnp.bfloat16)
     top_parts[top_count] = jnp.zeros(top_parts.shape[1:], jnp.bfloat16)
     for index in range(chunks):
         fetch_arrived(index).wait()
+        if index == min(1, chunks - 1):
+            for c in range(mids):
+                fetch_mid(c).start()
 
         @pl.loop(0, chunk, unroll=8)
         def _(slot):
@@ -352,47 +336,43 @@
         for line in range(lines_held):
             top_parts[base + line] = lanes_of(held[first_top + line])
 
-    for copy in small:
-        copy.wait()
+    for index in range(ahead):
+        for copy in fetch_leaves(index):
+            copy.start()
+    fetch_top.wait()
     stacked = jnp.concatenate([top_parts[tops[k]] for k in range(tops.shape[0])], axis=0)
-    near_top[...] = fold(dot(rows_of(top_held[...]), stacked))
+    parts[slots + 1] = lanes_of(fold(dot(rows_of(top_held[...]), stacked)))
     for c in range(mids):
         fetch_mid(c).wait()
 
     @pl.loop(0, mids, step=4)
     def _(start):
-        near = []
+        values = []
         for g in range(4):
-            c = start + g
-            stacked = jnp.concatenate([parts[pair[c, k]] for k in range(pair.shape[1])], axis=0)
-            value = fold(dot(mid_wide_held[c], stacked))
-            near.append(value + deep_dot(mid_transfer_held[c], near_top[...]))
+            blocks = [parts[pair[start + g, k]] for k in range(pair.shape[1])] + [parts[slots + 1]]
+            values.append(fold(dot(mid_wide_held[start + g], jnp.concatenate(blocks, axis=0))))
         for g in range(4):
-            down[start + g] = near[g]
-
-    @pl.loop(0, leaves, step=8)
-    def _(start):
-        terms = [deep_dot(transfer_held[start + g], down[parent[start + g]]) for g in range(8)]
-        for g in range(8):
-            back[start + g] = terms[g]
+            leaf_parts[slots + 1 + start + g] = lanes_of(values[g])
 
     point = lax.broadcasted_iota(jnp.int32, (points, ports), 0)
 
     def send(index):
         rows = group * points
-        target = out.at[pl.ds(pl.multiple_of(index * rows, rows), rows), :]
+        target = out.at[pl.ds(index * rows, rows), :]
         return pltpu.make_async_copy(out_held.at[index % 2], target, out_sem.at[index % 2])
 
-    for index in range(leaves // group):
+    for index in range(steps):
+        if index + ahead < steps:
+            for copy in fetch_leaves(index + ahead):
+                copy.start()
         for copy in fetch_leaves(index):
             copy.wait()
         values = []
         for g in range(group):
             leaf = index * group + g
-            stacked = jnp.concatenate(
-                [leaf_parts[pair_leaf[leaf, k]] for k in range(pair_leaf.shape[1])], axis=0
-            )
-            values.append(fold(dot(wide_held[leaf], stacked)) + back[leaf])
+            blocks = [leaf_parts[pair_leaf[leaf, k]] for k in range(pair_leaf.shape[1])]
+            blocks.append(leaf_parts[slots + 1 + parent[leaf]])
+            values.append(fold(dot(wide_held[leaf], jnp.concatenate(blocks, axis=0))))
         if index >= 2:
             send(index - 2).wait()
         for g in range(group):
@@ -400,19 +380,19 @@
             far = jnp.where(point < size[index * group + g], far, 0.0)
             out_held[index % 2, g * points : (g + 1) * points, :] = far
         send(index).start()
-    for index in range(max(0, leaves // group - 2), leaves // group):
+    for index in range(max(0, steps - 2), steps):
         send(index).wait()
 
 
 def tail(
     bounds, per_pair, groups, parent, pair, position, tops, size, pair_leaf, near_side, far_side, arrived,
-    mid_wide, mid_transfer, transfer, top_coupling, wide, basis
+    mid_wide, top_coupling, wide, basis
 ):
-    mids, _, mid_width = mid_wide.shape
+    mids = mid_wide.shape[0]
     leaves, points, _ = basis.shape
     slots, rank, ports = arrived.shape
     owners = slots // per_pair
-    group, chunk = 4, min(slots, 32)
+    group, chunk, ahead = 4, min(slots, 32), 3
     held = []
     for message in range(len(near_side)):
         batch = message // groups
@@ -421,30 +401,25 @@
     scratch = [((h, rank, ports), full) for h in held + held] + [
         ((2, chunk, rank, ports), full),
         (mid_wide.shape, half),
-        (mid_transfer.shape, half),
-        (transfer.shape, half),
         (top_coupling.shape[1:], full),
         (wide.shape, half),
         (basis.shape, half),
-        ((slots + 1, rank, 2 * ports), half),
+        ((slots + 2, rank, 2 * ports), half),
         ((owners + 1, rank, 2 * ports), half),
-        ((slots + 1, rank, 2 * ports), half),
-        ((rank, ports), full),
-        ((mids, rank, ports), full),
-        ((leaves, rank, ports), full),
+        ((slots + 1 + mids, rank, 2 * ports), half),
         ((2, group * points, ports), full),
     ]
-    semaphores = [2 * len(near_side), 2, mids, 3, leaves // group, leaves // group, 2]
+    semaphores = [(2 * len(near_side),), (2,), (mids,), (), (leaves // group,), (leaves // group,), (2,)]
     scalars = (parent, pair, position, tops, size, pair_leaf)
-    arrays = (*near_side, *far_side, arrived, mid_wide, mid_transfer, transfer, top_coupling, wide, basis)
+    arrays = (*near_side, *far_side, arrived, mid_wide, top_coupling, wide, basis)
     return pl.pallas_call(
-        functools.partial(tail_kernel, (bounds, per_pair, groups, chunk, group)),
+        functools.partial(tail_kernel, (bounds, per_pair, groups, chunk, group, ahead)),
         in_specs=[pl.BlockSpec(memory_space=pltpu.SMEM)] * len(scalars)
         + [pl.BlockSpec(memory_space=pl.ANY)] * len(arrays),
         out_specs=pl.BlockSpec(memory_space=pl.ANY),
         out_shape=jax.ShapeDtypeStruct((leaves * points, ports), full),
         scratch_shapes=[pltpu.VMEM(shape, dtype) for shape, dtype in scratch]
-        + [pltpu.SemaphoreType.DMA((n,)) for n in semaphores],
+        + [pltpu.SemaphoreType.DMA(n) for n in semaphores],
         compiler_params=params(60 * MIB),
         cost_estimate=cost(6 * 10**9, 2 * 10**7),
         name="tail",
@@ -478,40 +453,47 @@
         received.append(
             lax.ppermute(lifted, "cluster", [(c, c ^ (2 * d)) for c in range(per_cluster)])
         )
-    wide, basis_t, transfer_t, mid_wide, mid_transfer_t = prepare(
+    wide, basis_t, mid_wide = prepare(
         lifted, leaf_coupling, leaf_basis, leaf_transfer, mid_coupling, mid_transfer
     )
 
+    def spot_of(sender):
+        at_group, at_lane = sender // per_cluster, sender % per_cluster
+        line = (at_lane // 2) ^ (lane // 2)
+        return ((at_group ^ group) * 2 + ((at_lane ^ lane) & 1)) * lines + line
+
+    spot = spot_of(pair_mid // per_pair) * per_pair + pair_mid % per_pair
+    spot = jnp.where((pair_mid >= 0) & (pair_mid < slots), spot, slots)
+    wanted = lax.dynamic_slice_in_dim(top_pairs, lane, 1, 0)[0]
+    tops = jnp.where((wanted >= 0) & (wanted < owners), spot_of(wanted), owners)
+
+    own_messages, received[1], spot, tops, pair_leaf, mid_wide = lax.optimization_barrier(
+        (own_messages, received[1], spot, tops, pair_leaf, mid_wide)
+    )
     bounds = (0, 1, lines)
+    swap = [(c, c ^ 1) for c in range(per_cluster)]
     near_side, far_side = [], []
     for low, high in zip(bounds[:-1], bounds[1:]):
-        held = high - low
-        sizes = (held, per_cluster, up_rows, mids, rank, per_pair, groups)
+        sizes = (high - low, per_cluster, up_rows, mids, rank, per_pair, groups)
         messages = own_messages if low == 0 else select(sizes, group_at, lane_at, received[low:high])
         moved = [messages[0]]
         for d in range(1, groups):
             moved.append(lax.ppermute(messages[d], "group", [(g, g ^ d) for g in range(groups)]))
+        if high < lines:
+            near_side += moved
         if low == 0:
-            outgoing, moved, received[1:] = lax.optimization_barrier((outgoing, moved, received[1:]))
+            outgoing, near_side, received[1:] = lax.optimization_barrier(
+                (outgoing, near_side, received[1:])
+            )
             arrived = lax.all_to_all(outgoing, AXES, split_axis=0, concat_axis=0, tiled=True)
-        else:
-            moved, mid_wide = lax.optimization_barrier((moved, mid_wide))
-        near_side += moved
-        swap = [(c, c ^ 1) for c in range(per_cluster)]
-        far_side += [lax.ppermute(m, "cluster", swap) for m in moved]
-
-    def spot_of(sender):
-        at_group, at_lane = sender // per_cluster, sender % per_cluster
-        line = (at_lane // 2) ^ (lane // 2)
-        return ((at_group ^ group) * 2 + ((at_lane ^ lane) & 1)) * lines + line
-
-    spot = spot_of(pair_mid // per_pair) * per_pair + pair_mid % per_pair
-    spot = jnp.where((pair_mid >= 0) & (pair_mid < slots), spot, slots)
-    wanted = lax.dynamic_slice_in_dim(top_pairs, lane, 1, 0)[0]
-    tops = jnp.where((wanted >= 0) & (wanted < owners), spot_of(wanted), owners)
+            far_side = [lax.ppermute(m, "cluster", swap) for m in near_side]
+        if high == lines:
+            near_side += moved
+            far_side += [lax.ppermute(m, "cluster", swap) for m in moved]
+
     return tail(
         bounds, per_pair, groups, leaf_parent, spot, lane_at, tops, leaf_size, pair_leaf, near_side,
-        far_side, arrived, mid_wide, mid_transfer_t, transfer_t, top_coupling, wide, basis_t,
+        far_side, arrived, mid_wide, top_coupling, wide, basis_t,
     )
 
 

time: 115 us -> 113 us (0.983)
  waiting for transfers between devices: 48.3 us -> 51 us
  Pallas kernels: 41.2 us -> 39.4 us
  starting transfers between devices: 19.2 us -> 17.4 us
    ppermute x6, waiting for transfers between devices: 30.6 us -> 42 us  [body(): lax.ppermute(messages[d], 'group', [(g, g ^ d) for g in range(groups)])]
    ppermute x3, waiting for transfers between devices: 15.6 us -> 5.23 us  [body(): lax.ppermute(lifted, 'cluster', [(c, c ^ 2 * d) for c in range(per_cluste...]
    ppermute x0 -> x4, waiting for transfers between devices: none -> 3.43 us  [body(): far_side = [lax.ppermute(m, 'cluster', swap) for m in near_side]]
    ppermute x6, starting transfers between devices: 9.28 us -> 7.04 us  [body(): lax.ppermute(messages[d], 'group', [(g, g ^ d) for g in range(groups)])]
    pallas_call x1, Pallas kernels: 16.5 us -> 14.4 us  [tail(): pl.pallas_call(functools.partial(tail_kernel, (bounds, per_pair, groups,...]
    ppermute x8 -> x4, waiting for transfers between devices: 2.04 us -> 0.01 us  [body(): far_side += [lax.ppermute(m, 'cluster', swap) for m in moved]]
    ppermute x8 -> x4, starting transfers between devices: 1.74 us -> 0.15 us  [body(): far_side += [lax.ppermute(m, 'cluster', swap) for m in moved]]
    ppermute x3, starting transfers between devices: 4.39 us -> 5.74 us  [body(): lax.ppermute(lifted, 'cluster', [(c, c ^ 2 * d) for c in range(per_cluste...]
  transfers between devices with their start and end apart: 18 -> 18, of which waited for: 7 -> 10; matrix products, arithmetic and copies ran while one was open for 2% -> 2% of each run, Pallas kernels for 15% -> 16%
where the time goes in v1:
time: 113 us; the launch traced here: 111 us
  waiting for transfers between devices  51 us (45%)
  Pallas kernels  39.4 us (35%)
  starting transfers between devices  17.4 us (15%)
  local copies, waits for them, and re-layouts  2.32 us (2%)
  other arithmetic  1.22 us (1%)
    ppermute x6, waiting for transfers between devices, body(): lax.ppermute(messages[d], 'group', [(g, g ^ d) for g in range(groups)])  42 us
    pallas_call x1, Pallas kernels, tail(): pl.pallas_call(functools.partial(tail_kernel, (bounds, per_pair, groups,...  14.4 us
    pallas_call x1, Pallas kernels, prepare(): pl.pallas_call(prepare_kernel, grid=(steps,), in_specs=[pl.BlockSpec(memo...  12.3 us
    pallas_call x1, Pallas kernels, up_sweep(): pl.pallas_call(functools.partial(up_kernel, sizes), grid_spec=pltpu.Prefe...  7.35 us
    ppermute x6, starting transfers between devices, body(): lax.ppermute(messages[d], 'group', [(g, g ^ d) for g in range(groups)])  7.04 us
    ppermute x3, starting transfers between devices, body(): lax.ppermute(lifted, 'cluster', [(c, c ^ 2 * d) for c in range(per_cluste...  5.74 us
    ppermute x3, waiting for transfers between devices, body(): lax.ppermute(lifted, 'cluster', [(c, c ^ 2 * d) for c in range(per_cluste...  5.23 us
    ppermute x4, waiting for transfers between devices, body(): far_side = [lax.ppermute(m, 'cluster', swap) for m in near_side]  3.43 us
  transfers between devices with their start and end apart: 18, of which 10 were waited for; matrix products, arithmetic and copies ran while one was open for 2% of the time, Pallas kernels for 16%

profile of v1, /device:TPU:0, one launch (start us, length us, event | category | flops | bytes accessed | tf_op | source)
XLA Modules:
  0.0 111.5 jit_solution(10441778330275061082)
XLA Ops:
  0.0 7.4 %up_sweep.1 = (f32[32,64,128]{2,1,0:T(8,128)}, f32[584,128]{1,0:T(8,128)}, f32[5,64,128]{2,1,0:T(8,128)}, f32[5,64,128]{2,1,0:T(8,128)}, f32[5,64,128]{2,1,0:T(8,128)}, /*index=5*/f32[5,64,128]{2,1,0:T(8,128)}) custom-call(s32[32]{0:T(128)} %size.3, s32[32]{0:T(128)} %parent.3, s32[64]{0:T(128)} %slots.1, s32[1]{0:T(128)} %bitcast.group_at, ...), custom_call_target="tpu_custom_call" | custom-call | flops 1000000000 | bytes 10000000 | tf_op jit(solution)/shard_map/up_sweep/pallas_call | solution.py:119
  7.4 5.1 %collective-permute-start.5 = (f32[584,128]{1,0:T(8,128)}, f32[584,128]{1,0:T(8,128)S(1)}, u32[]{:S(2)}, u32[]{:S(2)}) collective-permute-start(f32[584,128]{1,0:T(8,128)} %get-tuple-element.39.after), channel_id=1, source_target_pairs={{0,6},{1,7},{2,4},{3,5},{4,2},{5,3},{6,0},{7,1},{8,14},{9,15},{10,... | collective-permute-start | bytes 897032 | tf_op jit(solution)/shard_map/ppermute | solution.py:454
  12.5 0.0 collective-permute-start.4
  12.5 0.6 collective-permute-start
  13.1 0.6 fusion.7.pair
  13.7 0.2 dynamic-slice_reduce_fusion
  13.9 12.3 %prepare.1 = (bf16[32,128,832]{2,1,0:T(8,128)(2,1)}, bf16[32,256,128]{2,1,0:T(8,128)(2,1)}, bf16[8,128,2112]{2,1,0:T(8,128)(2,1)}) custom-call(f32[584,128]{1,0:T(8,128)} %get-tuple-element.39.after, f32[32,64,768]{2,1,0:T(8,128)} %coupling.1, f32[32,64,256]{2,1,0:T(8,128)} %basis.3, f32[32,64,64]{2,1,0:T(8,128)} %transfer.3, f32[8,64,2048]{2,1,0:T(8,128)} %mid_coupling.1, ...), custom_call_target="tpu_custom_call" | custom-call | bytes 30000000 | tf_op jit(solution)/shard_map/prepare/pallas_call | solution.py:244
  26.2 0.6 and_select_fusion.3.tops
  26.8 5.2 %collective-permute-done.refs_0_ = f32[584,128]{1,0:T(8,128)S(1)} collective-permute-done((f32[584,128]{1,0:T(8,128)}, f32[584,128]{1,0:T(8,128)S(1)}, u32[]{:S(2)}, u32[]{:S(2)}) %collective-permute-start) | collective-permute-done | bytes 299040 | tf_op jit(solution)/shard_map/ppermute | solution.py:454
  32.0 1.5 %collective-permute-start.1 = (f32[5,64,128]{2,1,0:T(8,128)S(1)}, f32[5,64,128]{2,1,0:T(8,128)S(1)}, u32[]{:S(2)}, u32[]{:S(2)}) collective-permute-start(f32[5,64,128]{2,1,0:T(8,128)S(1)} %copy-done.16), channel_id=1, source_target_pairs={{0,8},{8,0},{16,24},{24,16},{1,9},{9,1},{17,25},{25,17},{2,10},{10... | collective-permute-start | bytes 491528 | tf_op jit(solution)/shard_map/ppermute | solution.py:481
  33.5 1.5 %collective-permute-start.2 = (f32[5,64,128]{2,1,0:T(8,128)S(1)}, f32[5,64,128]{2,1,0:T(8,128)}, u32[]{:S(2)}, u32[]{:S(2)}) collective-permute-start(f32[5,64,128]{2,1,0:T(8,128)S(1)} %copy-done.15), channel_id=1, source_target_pairs={{0,16},{8,24},{16,0},{24,8},{1,17},{9,25},{17,1},{25,9},{2,18},{10... | collective-permute-start | bytes 491528 | tf_op jit(solution)/shard_map/ppermute | solution.py:481
  35.1 0.0 copy-done.14
  35.1 0.5 collective-permute-start.3
  35.5 2.7 %spread.1 = f32[64,64,128]{2,1,0:T(8,128)} custom-call(s32[64]{0:T(128)} %send.1, f32[32,64,128]{2,1,0:T(8,128)} %get-tuple-element.44.coef), custom_call_target="tpu_custom_call" | custom-call | bytes 4000000 | tf_op jit(solution)/shard_map/spread/pallas_call | solution.py:157
  38.3 0.0 collective-permute-done.5.refs_2_
  38.3 0.0 collective-permute-done.4.refs_1_
  38.3 0.5 collective-permute-done.1.refs_1_
  38.8 3.6 %collective-permute-done.2.refs_2_ = f32[5,64,128]{2,1,0:T(8,128)} collective-permute-done((f32[5,64,128]{2,1,0:T(8,128)S(1)}, f32[5,64,128]{2,1,0:T(8,128)}, u32[]{:S(2)}, u32[]{:S(2)}) %collective-permute-start.2) | collective-permute-done | bytes 163872 | tf_op jit(solution)/shard_map/ppermute | solution.py:481
  42.4 0.0 collective-permute-done.3.refs_3_
  42.4 3.3 %all-to-all-start = ((f32[64,64,128]{2,1,0:T(8,128)}), f32[64,64,128]{2,1,0:T(8,128)S(1)}, u32[]{:S(2)}, u32[]{:S(2)}) async-start(f32[64,64,128]{2,1,0:T(8,128)} %spread.1), calls=%async_computation | async-start | bytes 4194304 | tf_op jit(solution)/shard_map/all_to_all | solution.py:488
  45.7 2.7 %select.31 = (f32[15,64,128]{2,1,0:T(8,128)}, f32[15,64,128]{2,1,0:T(8,128)}, f32[15,64,128]{2,1,0:T(8,128)}, f32[15,64,128]{2,1,0:T(8,128)}) custom-call(s32[1]{0:T(128)} %bitcast.group_at, s32[1]{0:T(128)} %bitcast.1.lane_at.position, f32[584,128]{1,0:T(8,128)} %copy-done.6, f32[584,128]{1,0:T(8,128)} %copy-done.5, f32[584,128]{1,0:T(8,128)} %copy-done.4), custom_call_target="tpu_custom_call" | custom-call | bytes 4000000 | tf_op jit(solution)/shard_map/select/pallas_call | solution.py:207
  48.4 1.8 %collective-permute-start.6 = (f32[15,64,128]{2,1,0:T(8,128)}, f32[15,64,128]{2,1,0:T(8,128)S(1)}, u32[]{:S(2)}, u32[]{:S(2)}) collective-permute-start(f32[15,64,128]{2,1,0:T(8,128)} %get-tuple-element.58), channel_id=1, source_target_pairs={{0,8},{8,0},{16,24},{24,16},{1,9},{9,1},{17,25},{25,17},{2,10},{10... | collective-permute-start | bytes 1474568 | tf_op jit(solution)/shard_map/ppermute | solution.py:481
  50.3 1.5 %collective-permute-start.7 = (f32[15,64,128]{2,1,0:T(8,128)}, f32[15,64,128]{2,1,0:T(8,128)S(1)}, u32[]{:S(2)}, u32[]{:S(2)}) collective-permute-start(f32[15,64,128]{2,1,0:T(8,128)} %get-tuple-element.59), channel_id=1, source_target_pairs={{0,16},{8,24},{16,0},{24,8},{1,17},{9,25},{17,1},{25,9},{2,18},{10... | collective-permute-start | bytes 1474568 | tf_op jit(solution)/shard_map/ppermute | solution.py:481
  51.7 0.3 collective-permute-start.8
  52.0 0.0 collective-permute-start.9
  52.0 0.5 collective-permute-start.10
  52.5 0.9 collective-permute-done.9.refs_8_
  53.4 0.1 collective-permute-start.13
  53.5 22.7 %collective-permute-done.6.refs_5_ = f32[15,64,128]{2,1,0:T(8,128)S(1)} collective-permute-done((f32[15,64,128]{2,1,0:T(8,128)}, f32[15,64,128]{2,1,0:T(8,128)S(1)}, u32[]{:S(2)}, u32[]{:S(2)}) %collective-permute-start.6) | collective-permute-done | bytes 491552 | tf_op jit(solution)/shard_map/ppermute | solution.py:481
  76.2 0.0 collective-permute-start.14
  76.2 3.0 %collective-permute-done.7.refs_6_ = f32[15,64,128]{2,1,0:T(8,128)S(1)} collective-permute-done((f32[15,64,128]{2,1,0:T(8,128)}, f32[15,64,128]{2,1,0:T(8,128)S(1)}, u32[]{:S(2)}, u32[]{:S(2)}) %collective-permute-start.7) | collective-permute-done | bytes 491552 | tf_op jit(solution)/shard_map/ppermute | solution.py:481
  79.2 0.0 collective-permute-start.15
  79.2 12.3 %collective-permute-done.8.refs_7_ = f32[15,64,128]{2,1,0:T(8,128)} collective-permute-done((f32[15,64,128]{2,1,0:T(8,128)}, f32[15,64,128]{2,1,0:T(8,128)}, u32[]{:S(2)}, u32[]{:S(2)}) %collective-permute-start.8) | collective-permute-done | bytes 491552 | tf_op jit(solution)/shard_map/ppermute | solution.py:481
  91.5 0.0 collective-permute-start.16
  91.5 0.0 collective-permute-done.10.refs_9_
  91.5 0.6 collective-permute-start.11
  92.0 0.1 copy-done.10
  92.1 1.6 %collective-permute-done.11.refs_10_ = f32[5,64,128]{2,1,0:T(8,128)S(1)} collective-permute-done((f32[5,64,128]{2,1,0:T(8,128)}, f32[5,64,128]{2,1,0:T(8,128)S(1)}, u32[]{:S(2)}, u32[]{:S(2)}) %collective-permute-start.11) | collective-permute-done | bytes 163872 | tf_op jit(solution)/shard_map/ppermute | solution.py:489
  93.8 0.1 collective-permute-start.12
  93.9 0.7 copy.15.pair_leaf
  94.6 0.9 collective-permute-done.12.refs_11_
  95.5 0.0 collective-permute-done.13.refs_12_
  95.5 0.0 collective-permute-done.14.refs_13_
  95.5 0.0 collective-permute-done.15.refs_14_
  95.5 0.0 collective-permute-done.16.refs_15_
  95.5 0.3 all-to-all-done.refs_16_
  95.8 1.3 %copy-done.1 = f32[64,64,128]{2,1,0:T(8,128)} copy-done((f32[64,64,128]{2,1,0:T(8,128)}, f32[64,64,128]{2,1,0:T(8,128)S(1)}, u32[]{:S(2)}) %copy-start.1) | copy-done | bytes 2097176
  97.1 14.4 %tail.1 = f32[8192,128]{1,0:T(8,128)} custom-call(s32[32]{0:T(128)} %parent.3, s32[8,32]{1,0:T(8,128)} %fusion.7.pair, s32[1]{0:T(128)} %bitcast.1.lane_at.position, s32[4]{0:T(128)} %and_select_fusion.3.tops, s32[32]{0:T(128)} %size.3, s32[32,12]{1,0:T(8,128)} %copy.15.pair_leaf, f32[5,64,128]{2,1,0:T(8,128)} %get-tuple-element.50.refs_0_, ...), custom_call_target="tpu_custom_call" | custom-call | flops 6000000000 | bytes 20000000 | tf_op jit(solution)/shard_map/tail/pallas_call | solution.py:415
  (31 shorter events, 0.1 us)
Async XLA Ops:
  0.0 13.7 %copy-start = (s32[8,4]{0,1:T(4,128)S(1)}, s32[8,4]{0,1:T(4,128)}, u32[]{:S(2)}) copy-start(s32[8,4]{0,1:T(4,128)} %param.26) | copy-start | bytes 388
  0.0 13.1 %copy-start.13 = (s32[8,32]{1,0:T(8,128)S(1)}, s32[8,32]{1,0:T(8,128)}, u32[]{:S(2)}) copy-start(s32[8,32]{1,0:T(8,128)} %param.24) | copy-start | bytes 3076
  7.4 30.9 %collective-permute-start.5 = (f32[584,128]{1,0:T(8,128)}, f32[584,128]{1,0:T(8,128)S(1)}, u32[]{:S(2)}, u32[]{:S(2)}) collective-permute-start(f32[584,128]{1,0:T(8,128)} %get-tuple-element.39.after), channel_id=1, source_target_pairs={{0,6},{1,7},{2,4},{3,5},{4,2},{5,3},{6,0},{7,1},{8,14},{9,15},{10,... | collective-permute-start | bytes 897032 | tf_op jit(solution)/shard_map/ppermute | solution.py:454
  12.5 25.8 %collective-permute-start.4 = (f32[584,128]{1,0:T(8,128)}, f32[584,128]{1,0:T(8,128)S(1)}, u32[]{:S(2)}, u32[]{:S(2)}) collective-permute-start(f32[584,128]{1,0:T(8,128)} %get-tuple-element.39.after), channel_id=1, source_target_pairs={{0,4},{1,5},{2,6},{3,7},{4,0},{5,1},{6,2},{7,3},{8,12},{9,13},{10,... | collective-permute-start | bytes 897032 | tf_op jit(solution)/shard_map/ppermute | solution.py:454
  12.5 19.6 %collective-permute-start = (f32[584,128]{1,0:T(8,128)}, f32[584,128]{1,0:T(8,128)S(1)}, u32[]{:S(2)}, u32[]{:S(2)}) collective-permute-start(f32[584,128]{1,0:T(8,128)} %get-tuple-element.39.after), channel_id=1, source_target_pairs={{0,2},{1,3},{2,0},{3,1},{4,6},{5,7},{6,4},{7,5},{8,10},{9,11},{10,... | collective-permute-start | bytes 897032 | tf_op jit(solution)/shard_map/ppermute | solution.py:454
  13.9 18.1 %copy-start.16 = (f32[5,64,128]{2,1,0:T(8,128)S(1)}, f32[5,64,128]{2,1,0:T(8,128)}, u32[]{:S(2)}) copy-start(f32[5,64,128]{2,1,0:T(8,128)} %get-tuple-element.46) | copy-start | bytes 491524
  13.9 19.6 %copy-start.15 = (f32[5,64,128]{2,1,0:T(8,128)S(1)}, f32[5,64,128]{2,1,0:T(8,128)}, u32[]{:S(2)}) copy-start(f32[5,64,128]{2,1,0:T(8,128)} %get-tuple-element.47) | copy-start | bytes 491524
  13.9 21.1 %copy-start.14 = (f32[5,64,128]{2,1,0:T(8,128)S(1)}, f32[5,64,128]{2,1,0:T(8,128)}, u32[]{:S(2)}) copy-start(f32[5,64,128]{2,1,0:T(8,128)} %get-tuple-element.48) | copy-start | bytes 491524
  26.2 25.8 %copy-start.7 = (f32[5,64,128]{2,1,0:T(8,128)S(1)}, f32[5,64,128]{2,1,0:T(8,128)}, u32[]{:S(2)}) copy-start(f32[5,64,128]{2,1,0:T(8,128)} %get-tuple-element.50.refs_0_) | copy-start | bytes 491524
  26.2 67.7 %copy-start.12 = (s32[32,12]{0,1:T(8,128)S(1)}, s32[32,12]{0,1:T(8,128)}, u32[]{:S(2)}) copy-start(s32[32,12]{0,1:T(8,128)} %param.21) | copy-start | bytes 4612
  32.0 13.7 %copy-start.6 = (f32[584,128]{1,0:T(8,128)}, f32[584,128]{1,0:T(8,128)S(1)}, u32[]{:S(2)}) copy-start(f32[584,128]{1,0:T(8,128)S(1)} %collective-permute-done.refs_0_) | copy-start | bytes 897028
  32.0 6.7 %collective-permute-start.1 = (f32[5,64,128]{2,1,0:T(8,128)S(1)}, f32[5,64,128]{2,1,0:T(8,128)S(1)}, u32[]{:S(2)}, u32[]{:S(2)}) collective-permute-start(f32[5,64,128]{2,1,0:T(8,128)S(1)} %copy-done.16), channel_id=1, source_target_pairs={{0,8},{8,0},{16,24},{24,16},{1,9},{9,1},{17,25},{25,17},{2,10},{10... | collective-permute-start | bytes 491528 | tf_op jit(solution)/shard_map/ppermute | solution.py:481
  33.5 8.8 %collective-permute-start.2 = (f32[5,64,128]{2,1,0:T(8,128)S(1)}, f32[5,64,128]{2,1,0:T(8,128)}, u32[]{:S(2)}, u32[]{:S(2)}) collective-permute-start(f32[5,64,128]{2,1,0:T(8,128)S(1)} %copy-done.15), channel_id=1, source_target_pairs={{0,16},{8,24},{16,0},{24,8},{1,17},{9,25},{17,1},{25,9},{2,18},{10... | collective-permute-start | bytes 491528 | tf_op jit(solution)/shard_map/ppermute | solution.py:481
  35.1 7.3 %collective-permute-start.3 = (f32[5,64,128]{2,1,0:T(8,128)S(1)}, f32[5,64,128]{2,1,0:T(8,128)}, u32[]{:S(2)}, u32[]{:S(2)}) collective-permute-start(f32[5,64,128]{2,1,0:T(8,128)S(1)} %copy-done.14), channel_id=1, source_target_pairs={{0,24},{8,16},{16,8},{24,0},{1,25},{9,17},{17,9},{25,1},{2,26},{10... | collective-permute-start | bytes 491528 | tf_op jit(solution)/shard_map/ppermute | solution.py:481
  38.3 7.4 %copy-start.4 = (f32[584,128]{1,0:T(8,128)}, f32[584,128]{1,0:T(8,128)S(1)}, u32[]{:S(2)}) copy-start(f32[584,128]{1,0:T(8,128)S(1)} %collective-permute-done.5.refs_2_) | copy-start | bytes 897028
  38.3 7.4 %copy-start.5 = (f32[584,128]{1,0:T(8,128)}, f32[584,128]{1,0:T(8,128)S(1)}, u32[]{:S(2)}) copy-start(f32[584,128]{1,0:T(8,128)S(1)} %collective-permute-done.4.refs_1_) | copy-start | bytes 897028
  38.7 57.1 %copy-start.8 = (f32[5,64,128]{2,1,0:T(8,128)}, f32[5,64,128]{2,1,0:T(8,128)S(1)}, u32[]{:S(2)}) copy-start(f32[5,64,128]{2,1,0:T(8,128)S(1)} %collective-permute-done.1.refs_1_) | copy-start | bytes 491524
  42.4 53.4 %all-to-all-start = ((f32[64,64,128]{2,1,0:T(8,128)}), f32[64,64,128]{2,1,0:T(8,128)S(1)}, u32[]{:S(2)}, u32[]{:S(2)}) async-start(f32[64,64,128]{2,1,0:T(8,128)} %spread.1), calls=%async_computation | async-start | bytes 4194304 | tf_op jit(solution)/shard_map/all_to_all | solution.py:488
  48.4 27.8 %collective-permute-start.6 = (f32[15,64,128]{2,1,0:T(8,128)}, f32[15,64,128]{2,1,0:T(8,128)S(1)}, u32[]{:S(2)}, u32[]{:S(2)}) collective-permute-start(f32[15,64,128]{2,1,0:T(8,128)} %get-tuple-element.58), channel_id=1, source_target_pairs={{0,8},{8,0},{16,24},{24,16},{1,9},{9,1},{17,25},{25,17},{2,10},{10... | collective-permute-start | bytes 1474568 | tf_op jit(solution)/shard_map/ppermute | solution.py:481
  50.3 28.9 %collective-permute-start.7 = (f32[15,64,128]{2,1,0:T(8,128)}, f32[15,64,128]{2,1,0:T(8,128)S(1)}, u32[]{:S(2)}, u32[]{:S(2)}) collective-permute-start(f32[15,64,128]{2,1,0:T(8,128)} %get-tuple-element.59), channel_id=1, source_target_pairs={{0,16},{8,24},{16,0},{24,8},{1,17},{9,25},{17,1},{25,9},{2,18},{10... | collective-permute-start | bytes 1474568 | tf_op jit(solution)/shard_map/ppermute | solution.py:481
  51.7 39.7 %collective-permute-start.8 = (f32[15,64,128]{2,1,0:T(8,128)}, f32[15,64,128]{2,1,0:T(8,128)}, u32[]{:S(2)}, u32[]{:S(2)}) collective-permute-start(f32[15,64,128]{2,1,0:T(8,128)} %get-tuple-element.60), channel_id=1, source_target_pairs={{0,24},{8,16},{16,8},{24,0},{1,25},{9,17},{17,9},{25,1},{2,26},{10... | collective-permute-start | bytes 1474568 | tf_op jit(solution)/shard_map/ppermute | solution.py:481
  52.0 1.4 %collective-permute-start.9 = (f32[5,64,128]{2,1,0:T(8,128)S(1)}, f32[5,64,128]{2,1,0:T(8,128)S(1)}, u32[]{:S(2)}, u32[]{:S(2)}) collective-permute-start(f32[5,64,128]{2,1,0:T(8,128)S(1)} %copy-done.7), channel_id=1, source_target_pairs={{0,1},{1,0},{2,3},{3,2},{4,5},{5,4},{6,7},{7,6},{8,9},{9,8},{10,11... | collective-permute-start | bytes 491528 | tf_op jit(solution)/shard_map/ppermute | solution.py:489
  52.0 39.5 %collective-permute-start.10 = (f32[5,64,128]{2,1,0:T(8,128)S(1)}, f32[5,64,128]{2,1,0:T(8,128)S(1)}, u32[]{:S(2)}, u32[]{:S(2)}) collective-permute-start(f32[5,64,128]{2,1,0:T(8,128)S(1)} %collective-permute-done.1.refs_1_), channel_id=1, source_target_pairs={{0,1},{1,0},{2,3},{3,2},{4,5},{5,4},{6,7},{7,6},{8,9},{9,8},{10,11... | collective-permute-start | bytes 491528 | tf_op jit(solution)/shard_map/ppermute | solution.py:489
  53.4 38.1 %copy-start.9 = (f32[5,64,128]{2,1,0:T(8,128)}, f32[5,64,128]{2,1,0:T(8,128)S(1)}, u32[]{:S(2)}) copy-start(f32[5,64,128]{2,1,0:T(8,128)S(1)} %collective-permute-done.9.refs_8_) | copy-start | bytes 491524
  53.4 42.1 %collective-permute-start.13 = (f32[15,64,128]{2,1,0:T(8,128)}, f32[15,64,128]{2,1,0:T(8,128)}, u32[]{:S(2)}, u32[]{:S(2)}) collective-permute-start(f32[15,64,128]{2,1,0:T(8,128)} %get-tuple-element.57.refs_4_), channel_id=1, source_target_pairs={{0,1},{1,0},{2,3},{3,2},{4,5},{5,4},{6,7},{7,6},{8,9},{9,8},{10,11... | collective-permute-start | bytes 1474568 | tf_op jit(solution)/shard_map/ppermute | solution.py:492
  76.2 19.6 %copy-start.2 = (f32[15,64,128]{2,1,0:T(8,128)}, f32[15,64,128]{2,1,0:T(8,128)S(1)}, u32[]{:S(2)}) copy-start(f32[15,64,128]{2,1,0:T(8,128)S(1)} %collective-permute-done.6.refs_5_) | copy-start | bytes 1474564
  76.2 19.3 %collective-permute-start.14 = (f32[15,64,128]{2,1,0:T(8,128)S(1)}, f32[15,64,128]{2,1,0:T(8,128)}, u32[]{:S(2)}, u32[]{:S(2)}) collective-permute-start(f32[15,64,128]{2,1,0:T(8,128)S(1)} %collective-permute-done.6.refs_5_), channel_id=1, source_target_pairs={{0,1},{1,0},{2,3},{3,2},{4,5},{5,4},{6,7},{7,6},{8,9},{9,8},{10,11... | collective-permute-start | bytes 1474568 | tf_op jit(solution)/shard_map/ppermute | solution.py:492
  79.2 16.6 %copy-start.3 = (f32[15,64,128]{2,1,0:T(8,128)}, f32[15,64,128]{2,1,0:T(8,128)S(1)}, u32[]{:S(2)}) copy-start(f32[15,64,128]{2,1,0:T(8,128)S(1)} %collective-permute-done.7.refs_6_) | copy-start | bytes 1474564
  79.2 16.3 %collective-permute-start.15 = (f32[15,64,128]{2,1,0:T(8,128)S(1)}, f32[15,64,128]{2,1,0:T(8,128)}, u32[]{:S(2)}, u32[]{:S(2)}) collective-permute-start(f32[15,64,128]{2,1,0:T(8,128)S(1)} %collective-permute-done.7.refs_6_), channel_id=1, source_target_pairs={{0,1},{1,0},{2,3},{3,2},{4,5},{5,4},{6,7},{7,6},{8,9},{9,8},{10,11... | collective-permute-start | bytes 1474568 | tf_op jit(solution)/shard_map/ppermute | solution.py:492
  91.5 4.1 %collective-permute-start.16 = (f32[15,64,128]{2,1,0:T(8,128)}, f32[15,64,128]{2,1,0:T(8,128)}, u32[]{:S(2)}, u32[]{:S(2)}) collective-permute-start(f32[15,64,128]{2,1,0:T(8,128)} %collective-permute-done.8.refs_7_), channel_id=1, source_target_pairs={{0,1},{1,0},{2,3},{3,2},{4,5},{5,4},{6,7},{7,6},{8,9},{9,8},{10,11... | collective-permute-start | bytes 1474568 | tf_op jit(solution)/shard_map/ppermute | solution.py:492
  91.5 0.7 copy-start.10
  91.5 2.3 %collective-permute-start.11 = (f32[5,64,128]{2,1,0:T(8,128)}, f32[5,64,128]{2,1,0:T(8,128)S(1)}, u32[]{:S(2)}, u32[]{:S(2)}) collective-permute-start(f32[5,64,128]{2,1,0:T(8,128)} %collective-permute-done.2.refs_2_), channel_id=1, source_target_pairs={{0,1},{1,0},{2,3},{3,2},{4,5},{5,4},{6,7},{7,6},{8,9},{9,8},{10,11... | collective-permute-start | bytes 491528 | tf_op jit(solution)/shard_map/ppermute | solution.py:489
  93.8 2.1 %copy-start.11 = (f32[5,64,128]{2,1,0:T(8,128)}, f32[5,64,128]{2,1,0:T(8,128)S(1)}, u32[]{:S(2)}) copy-start(f32[5,64,128]{2,1,0:T(8,128)S(1)} %collective-permute-done.11.refs_10_) | copy-start | bytes 491524
  93.8 1.7 %collective-permute-start.12 = (f32[5,64,128]{2,1,0:T(8,128)}, f32[5,64,128]{2,1,0:T(8,128)}, u32[]{:S(2)}, u32[]{:S(2)}) collective-permute-start(f32[5,64,128]{2,1,0:T(8,128)} %collective-permute-done.3.refs_3_), channel_id=1, source_target_pairs={{0,1},{1,0},{2,3},{3,2},{4,5},{5,4},{6,7},{7,6},{8,9},{9,8},{10,11... | collective-permute-start | bytes 491528 | tf_op jit(solution)/shard_map/ppermute | solution.py:489
  95.8 1.3 %copy-start.1 = (f32[64,64,128]{2,1,0:T(8,128)}, f32[64,64,128]{2,1,0:T(8,128)S(1)}, u32[]{:S(2)}) copy-start(f32[64,64,128]{2,1,0:T(8,128)S(1)} %all-to-all-done.refs_16_) | copy-start | bytes 6291460
